TPU v7x, 256 devices: a whole 4x4x8 slice. The times are simulated.
256 devices in a mesh: grid: 32 (over y_hi, z, core), chan: 8 (over x, y_lo).
Axes of the slice: x: 4, y: 4 (y_hi: 2, y_lo: 2; y = y_hi * 2 + y_lo), z: 8, core: 2. Of those that a mesh axis runs over, the one named last changes fastest.
Arguments:
- activations: bfloat16 [256, 32, 8, 16, 128], P('chan', 'grid'), may hold values from -6 to 6
- grad_out: bfloat16 [256, 32, 16, 128], P('chan', 'grid'), may hold values from -6 to 6
- weight: bfloat16 [27, 256, 256], P(None, 'chan'), may hold values from -0.078125 to 0.078125
Outputs:
- grad_act: bfloat16 [256, 32, 8, 16, 128], P('chan', 'grid')
- grad_weight: float32 [27, 256, 256], P(None, 'chan')
All inputs are finite; a program needn't handle non-finite values.
Results may differ from a plain program's by a relative error of at most 0.001.
Values may be sent and summed in bfloat16 or wider, within the bound.
A program may use at most 64 MiB of HBM per device.

v0:
```python
import math

import jax
import jax.numpy as jnp
from jax import lax
from jax.sharding import PartitionSpec as P


def shifted_2(block, axis, distance):
    devices = range(lax.axis_size(axis))
    route = [(i - distance, i) for i in devices if i - distance in devices]
    return lax.ppermute(block, axis, route)


def parity_taps(parity):
    if parity == 0:
        return [(1, 0)]
    return [(2, 0), (0, 1)]


def tap_parity(tap):
    if tap == 1:
        return (0, 0)
    if tap == 2:
        return (1, 0)
    return (1, 1)


def shifted_grads(grad_cells, rim_plane):
    result = {}
    for step_x in range(2):
        if step_x == 0:
            x_shifted = grad_cells
        else:
            x_shifted = jnp.concatenate([grad_cells[:, 1:], rim_plane[:, None]], 1)
        for step_y in range(2):
            if step_y == 0:
                y_shifted = x_shifted
            else:
                y_shifted = jnp.concatenate(
                    [x_shifted[:, :, 1:], jnp.zeros_like(x_shifted[:, :, :1])], 2
                )
            for step_z in range(2):
                if step_z == 0:
                    z_shifted = y_shifted
                else:
                    z_shifted = jnp.concatenate(
                        [y_shifted[:, :, :, 1:], jnp.zeros_like(y_shifted[:, :, :, :1])], 3
                    )
                result[step_x, step_y, step_z] = z_shifted
    return result


def on_device(activations, grad_out, weight):
    cin_dev, planes, parities, out_y, out_z = activations.shape
    count_out = planes * out_y * out_z
    scale_norm = 1.0 / math.sqrt(count_out * lax.axis_size("grid"))
    front_plane = shifted_2(activations[:, planes - 1 : planes, 4:8], "grid", 1)
    act_before = jnp.concatenate([front_plane, activations[:, : planes - 1, 4:8]], 1)
    gathered = lax.all_gather(grad_out, "chan", axis=0, tiled=True)
    rim_whole = shifted_2(gathered[:, 0], "grid", -1)
    piece_rows = gathered.shape[0]
    shifted = shifted_grads(gathered, rim_whole)
    blocks = []
    for parity in range(8):
        par_x, par_y, par_z = (parity // 4, parity // 2 % 2, parity % 2)
        block_sum = jnp.zeros((cin_dev, count_out), jnp.float32)
        for tap_x, step_x in parity_taps(par_x):
            for tap_y, step_y in parity_taps(par_y):
                for tap_z, step_z in parity_taps(par_z):
                    window = shifted[step_x, step_y, step_z].reshape(piece_rows, count_out)
                    block_sum = block_sum + jnp.dot(
                        weight[tap_x * 9 + tap_y * 3 + tap_z],
                        window,
                        preferred_element_type=jnp.float32,
                    )
        blocks.append(block_sum.reshape(cin_dev, planes, out_y, out_z))
    totals = jnp.stack(blocks, 2)
    tap_list = []
    for tap_index in range(27):
        tap_x = tap_index // 9
        par_x, step_x = tap_parity(tap_x)
        par_y, step_y = tap_parity(tap_index // 3 % 3)
        par_z, step_z = tap_parity(tap_index % 3)
        par_index = 4 * par_x + 2 * par_y + par_z
        if tap_x == 0:
            act_slab = act_before[:, :, par_index - 4]
            grad_slab = shifted[0, step_y, step_z]
        else:
            act_slab = activations[:, :, par_index]
            grad_slab = shifted[step_x, step_y, step_z]
        tap_list.append(
            jnp.einsum("cxyz,oxyz->co", act_slab, grad_slab, preferred_element_type=jnp.float32)
        )
    tap_terms = jnp.stack(tap_list, 0)
    grad_w = tap_terms
    totals, grad_w = (totals, grad_w)
    grad_act = totals.astype(jnp.bfloat16)
    grad_weight = lax.psum(grad_w, "grid") * scale_norm
    return (grad_act, grad_weight)


def solution(mesh):
    placed = (
        P("chan", "grid", None, None, None),
        P("chan", "grid", None, None),
        P(None, "chan", None),
    )
    return jax.shard_map(
        on_device,
        mesh=mesh,
        in_specs=placed,
        out_specs=(P("chan", "grid", None, None, None), P(None, "chan", None)),
        check_vma=False,
    )
```

profile of v0, /device:TPU:1, one launch (start us, length us, event | category | flops | bytes accessed | tf_op | source)
XLA Modules:
  0.0 415.9 jit_solution(3259047934980850593)
XLA Ops:
  11.0 4.9 %collective-permute-start.1 = (bf16[32,1,4,16,128]{4,0,3,2,1:T(8,128)(2,1)}, bf16[32,1,4,16,128]{4,0,3,2,1:T(8,128)(2,1)}, u32[]{:S(2)}, u32[]{:S(2)}) collective-permute-start(bf16[32,1,4,16,128]{4,0,3,2,1:T(8,128)(2,1)} %copy.42), channel_id=1, source_target_pairs={{0,8},{8,16},{16,24},{24,32},{32,40},{40,48},{48,56},{56,64},{64,7... | collective-permute-start | bytes 1572872 | tf_op jit(solution)/shard_map/ppermute | solution.py:12
  16.9 34.0 %all-gather.2.cloned.1.call-done = bf16[256,1,16,128]{3,0,2,1:T(8,128)(2,1)} async-done(((bf16[32,1,16,128]{3,0,2,1:T(8,128)(2,1)}), bf16[256,1,16,128]{3,0,2,1:T(8,128)(2,1)}) %all-gather.2.cloned.1.call-update) | async-done | bytes 1048592 | tf_op jit(solution)/shard_map/all_gather | solution.py:60
  54.2 1.8 fusion.105
  57.9 1.9 fusion.99
  65.7 2.4 copy.93
  68.1 2.4 copy.95
  70.5 1.9 fusion.86
  74.2 1.9 fusion.57
  76.1 2.0 fusion.56
  78.2 1.9 fusion.55
  80.1 1.9 fusion.54
  82.0 1.9 fusion.53
  84.0 1.9 fusion.52
  85.9 1.9 fusion.51
  87.8 1.9 fusion.50
  89.8 1.9 fusion.49
  119.3 7.8 %collective-permute-start = (bf16[256,16,128]{2,0,1:T(8,128)(2,1)S(1)}, bf16[256,16,128]{2,0,1:T(8,128)(2,1)S(1)}, u32[]{:S(2)}, u32[]{:S(2)}) collective-permute-start(bf16[256,16,128]{2,0,1:T(8,128)(2,1)S(1)} %bitcast.519), channel_id=1, source_target_pairs={{8,0},{16,8},{24,16},{32,24},{40,32},{48,40},{56,48},{64,56},{72,6... | collective-permute-start | bytes 3145736 | tf_op jit(solution)/shard_map/ppermute | solution.py:12
  127.2 1.8 fusion.9
  136.4 1.9 fusion.3
  138.2 237.4 %all-reduce.8.cloned.1.call-done = f32[27,32,256]{2,1,0:T(8,128)} async-done(((f32[27,32,256]{2,1,0:T(8,128)}), f32[27,32,256]{2,1,0:T(8,128)}) %all-reduce.8.cloned.1.call-update) | async-done | bytes 884752 | tf_op jit(solution)/shard_map/psum | solution.py:99
  375.6 2.2 broadcast_multiply_fusion
  385.5 2.4 copy.51
  389.2 1.8 convolution_bitcast_fusion.8
  406.5 2.6 copy.41
  (131 shorter events, 76.7 us)
Async XLA Ops:
  7.2 43.8 %all-gather.2.cloned.1.call-start = ((), (), s32[]{:S(2)}) async-start(), calls=%async_computation | async-start | bytes 1179648 | tf_op jit(solution)/shard_map/all_gather | solution.py:60
  8.8 1.0 slice-start
  8.8 7.1 %copy-start.6 = (bf16[32,1,8,16,128]{4,3,2,1,0:T(8,128)(2,1)S(1)}, bf16[32,1,8,16,128]{4,3,2,1,0:T(8,128)(2,1)}, u32[]{:S(2)}) copy-start(bf16[32,1,8,16,128]{4,3,2,1,0:T(8,128)(2,1)} %param.3) | copy-start | bytes 3145732
  8.9 366.8 %all-reduce.8.cloned.1.call-start = ((), (), s32[]{:S(2)}) async-start(), calls=%async_computation.1 | async-start | bytes 1769472 | tf_op jit(solution)/shard_map/psum | solution.py:99
  11.0 63.2 %collective-permute-start.1 = (bf16[32,1,4,16,128]{4,0,3,2,1:T(8,128)(2,1)}, bf16[32,1,4,16,128]{4,0,3,2,1:T(8,128)(2,1)}, u32[]{:S(2)}, u32[]{:S(2)}) collective-permute-start(bf16[32,1,4,16,128]{4,0,3,2,1:T(8,128)(2,1)} %copy.42), channel_id=1, source_target_pairs={{0,8},{8,16},{16,24},{24,32},{32,40},{40,48},{48,56},{56,64},{64,7... | collective-permute-start | bytes 1572872 | tf_op jit(solution)/shard_map/ppermute | solution.py:12
  57.9 3.8 copy-start
  70.4 3.8 copy-start.2
  76.1 4.0 copy-start.1
  91.7 1.0 copy-start.8
  93.8 1.0 copy-start.9
  94.8 1.0 copy-start.23
  103.1 1.0 copy-start.7
  104.1 1.0 copy-start.22
  109.3 1.2 copy-start.4
  110.6 2.0 copy-start.5
  116.8 1.3 copy-start.3
  119.3 7.9 %copy-start.10 = (f32[32,2048]{1,0:T(8,128)S(1)}, f32[32,2048]{1,0:T(8,128)}, u32[]{:S(2)}) copy-start(f32[32,2048]{1,0:T(8,128)} %fusion.91) | copy-start | bytes 786436
  119.3 9.7 %copy-start.12 = (f32[32,2048]{1,0:T(8,128)S(1)}, f32[32,2048]{1,0:T(8,128)}, u32[]{:S(2)}) copy-start(f32[32,2048]{1,0:T(8,128)} %fusion.86) | copy-start | bytes 786436
  119.3 258.4 %collective-permute-start = (bf16[256,16,128]{2,0,1:T(8,128)(2,1)S(1)}, bf16[256,16,128]{2,0,1:T(8,128)(2,1)S(1)}, u32[]{:S(2)}, u32[]{:S(2)}) collective-permute-start(bf16[256,16,128]{2,0,1:T(8,128)(2,1)S(1)} %bitcast.519), channel_id=1, source_target_pairs={{8,0},{16,8},{24,16},{32,24},{40,32},{48,40},{56,48},{64,56},{72,6... | collective-permute-start | bytes 3145736 | tf_op jit(solution)/shard_map/ppermute | solution.py:12
  129.0 1.2 copy-start.11
  393.7 1.5 copy-start.19
  397.3 1.0 copy-start.18
  400.1 1.0 copy-start.20
  400.1 1.1 copy-start.21
  (6 other events, 5.7 us)
Sparse Core Ops, SparseCore 0:
  10.4 40.5 all-gather.1
  110.5 265.1 all-reduce.7
where the time goes:
time: 419 us; the launch traced here: 416 us
  waiting for transfers between devices  271 us (65%)
  matrix products  77 us (18%)
  local copies, waits for them, and re-layouts  38 us (9%)
  between operations  14.5 us (3%)
  starting transfers between devices  12.8 us (3%)
    psum x1, waiting for transfers between devices, on_device(): grad_weight = lax.psum(grad_w, 'grid') * scale_norm  237 us
    dot_general x27, matrix products, on_device(): jnp.dot(weight[tap_x * 9 + tap_y * 3 + tap_z], window, preferred_element_...  40.9 us
    dot_general x27, matrix products, on_device(): jnp.einsum('cxyz,oxyz->co', act_slab, grad_slab, preferred_element_type=j...  36.1 us
    all_gather x1, waiting for transfers between devices, on_device(): gathered = lax.all_gather(grad_out, 'chan', axis=0, tiled=True)  34 us
    unnamed x72, local copies, waits for them, and re-layouts  25.9 us
    ppermute x2, starting transfers between devices, shifted_2(): return lax.ppermute(block, axis, route)  12.7 us
  transfers between devices with their start and end apart: 4, of which 2 were waited for; matrix products, arithmetic and copies ran while one was open for 11% of the time, Pallas kernels for 0%

commit v1 on v0

v1 whole, which is shorter than its diff:
```python
import math

import jax
import jax.numpy as jnp
from jax import lax
from jax.experimental import pallas as pl
from jax.experimental.pallas import tpu as pltpu
from jax.sharding import PartitionSpec as P

MESH = pl.DeviceIdType.MESH
F32, BF16 = jnp.float32, jnp.bfloat16
NX, NYL, NZ, NYH = 4, 2, 8, 2
Y, Z = 16, 128
CELLS = Y * Z
PAD = 32
SPAN = 240.0


def tap_of(par, step):
    if par == 0:
        return 1 if step == 0 else None
    return 2 if step == 0 else 0


def taps_of_shift(shift):
    found = []
    for par in range(8):
        bits = (par // 4, par // 2 % 2, par % 2)
        taps = [tap_of(b, s) for b, s in zip(bits, shift)]
        if None not in taps:
            found.append((par, 9 * taps[0] + 3 * taps[1] + taps[2]))
    return found


SHIFTS = [(sx, sy, sz) for sx in range(2) for sy in range(2) for sz in range(2)]


def encode(values):
    largest = jnp.max(jnp.abs(values), axis=1, keepdims=True)
    scale = jnp.maximum((largest * 1.01).astype(BF16).astype(F32), 1e-30)
    level = values * (SPAN / scale)
    power = jnp.exp2(jnp.abs(level) - SPAN / 2)
    power = jnp.where(values < 0, -power, power)
    row = lax.broadcasted_iota(jnp.int32, values.shape, 1)
    return jnp.where(row >= 27, scale, power).astype(BF16)


def decode(codes):
    codes = codes.astype(F32)
    scale = codes[:, 27:28] * (1.0 / SPAN)
    level = (jnp.log2(jnp.abs(codes)) + SPAN / 2) * scale
    return jnp.where(codes < 0, -level, level)


def kernel(
    norm, act_ref, grad_ref, weight_ref, out_act, out_w,
    rows32, acts, grads, dense, terms, from_mate, rs_own, rs_out, rs_in, ag, final,
    send_own, recv_own, send_rim, recv_rim, mate_send, mate_recv,
    rs_send, rs_recv, ag_send, ag_recv, fw_send, fw_recv,
):
    g, chan = lax.axis_index("grid"), lax.axis_index("chan")
    yh, z, core = g // (2 * NZ), (g // 2) % NZ, g % 2
    x, yl = chan // NYL, chan % NYL
    w = yh * NZ + z

    def chan_of(dx, dy):
        return lax.rem(x + dx, NX) * NYL + lax.rem(yl + dy, NYL)

    def at_chan(dx, dy):
        return (g, chan_of(dx, dy))

    mate = (g + 1 - 2 * core, chan)
    before = (jnp.maximum(g - 1, 0), chan)

    def peer_w(d):
        a, k = d // NZ, d % NZ
        return lax.rem(yh + a, NYH) * NZ + lax.rem(z + k, NZ)

    def peer(d):
        return (peer_w(d) * 2 + core, chan)

    has_rim = jnp.logical_and(core == 1, g < 2 * NZ * NYH - 1)
    gives_rim = jnp.logical_and(core == 0, g > 0)

    barrier = pltpu.get_barrier_semaphore()
    near = [at_chan(1, 0), at_chan(3, 0), at_chan(2, 0), at_chan(0, 1), mate]
    near += [peer(d) for d in range(1, NZ * NYH)]
    for device in near:
        pl.semaphore_signal(barrier, inc=1, device_id=device, device_id_type=MESH)

    @pl.when(gives_rim)
    def _():
        pl.semaphore_signal(barrier, inc=1, device_id=before, device_id_type=MESH)

    @pl.when(has_rim)
    def _():
        pl.semaphore_signal(barrier, inc=1, device_id=(g + 1, chan), device_id_type=MESH)

    def shard(plane, dx, dy):
        start = pl.multiple_of(chan_of(dx, dy) * 32, 32)
        return grads.at[plane, 0, pl.ds(start, 32), pl.ds(0, CELLS)]

    rows32[0 : 32 * Y] = grad_ref[:, 0].astype(F32).reshape(32 * Y, Z)
    start_own = pl.multiple_of(chan * 32, 32)
    for j in range(Y):
        grads[0, 0, pl.ds(start_own, 32), j * Z : (j + 1) * Z] = rows32[
            pl.ds(j, 32, stride=Y)
        ].astype(BF16)

    rim_partners = jnp.logical_or(gives_rim, has_rim).astype(jnp.int32)
    pl.semaphore_wait(barrier, len(near) + rim_partners)

    def copy(src, dst, send, recv, device):
        return pltpu.make_async_remote_copy(
            src_ref=src, dst_ref=dst, send_sem=send, recv_sem=recv,
            device_id=device, device_id_type=MESH,
        )

    def gather_copies(plane, send, recv):
        def one(n, dx, dy, slot, device):
            return copy(
                shard(plane, dx, dy), shard(plane, dx, dy), send.at[n], recv.at[slot], device
            )

        own = [
            one(0, 0, 0, 1, at_chan(0, 1)),
            one(1, 0, 0, 6, at_chan(1, 0)),
            one(2, 0, 0, 2, at_chan(3, 0)),
            one(3, 0, 0, 4, at_chan(2, 0)),
        ]
        from_y = [one(4, 0, 1, 7, at_chan(1, 0)), one(5, 0, 1, 3, at_chan(3, 0))]
        from_x2 = [one(6, 2, 0, 5, at_chan(0, 1))]
        return own, from_y, from_x2

    def wait_shard(plane, recv, dx, dy):
        ref = shard(plane, dx, dy)
        pltpu.make_async_copy(ref, ref, recv.at[dx * 2 + dy]).wait()

    def to_core0(dx, dy):
        n = dx * 2 + dy
        return copy(
            shard(0, dx, dy), shard(1, dx, dy), mate_send.at[n], recv_rim.at[n], mate
        )

    def give_core0(dx, dy):
        @pl.when(core == 1)
        def _():
            to_core0(dx, dy).start()

    own, from_y, from_x2 = gather_copies(0, send_own, recv_own)
    rim_own, rim_from_y, rim_from_x2 = gather_copies(1, send_rim, recv_rim)
    rim_first = copy(
        shard(0, 0, 0), shard(1, 0, 0), mate_send.at[0], recv_rim.at[0], before
    )

    for c in own:
        c.start()
    give_core0(0, 0)

    @pl.when(gives_rim)
    def _():
        rim_first.start()

    for plane in range(2):
        for sz in range(2):
            grads[plane, sz, :, CELLS:] = jnp.zeros((256, Z), BF16)

    @pl.when(g == 2 * NZ * NYH - 1)
    def _():
        grads[1, 0, :, 0:CELLS] = jnp.zeros((256, CELLS), BF16)

    terms[...] = jnp.zeros_like(terms)

    for par in range(8):
        rows32[par * 32 * Y : (par + 1) * 32 * Y] = (
            act_ref[:, 0, par].astype(F32).reshape(32 * Y, Z)
        )
    for j in range(Y):
        acts[:, j * Z : (j + 1) * Z] = rows32[pl.ds(j, 256, stride=Y)].astype(BF16)

    wait_shard(0, recv_own, 0, 1)
    for c in from_y:
        c.start()
    give_core0(0, 1)

    @pl.when(has_rim)
    def _():
        wait_shard(1, recv_rim, 0, 0)
        for c in rim_own:
            c.start()

    wait_shard(0, recv_own, 1, 0)
    give_core0(1, 0)
    wait_shard(0, recv_own, 3, 0)
    give_core0(3, 0)
    wait_shard(0, recv_own, 2, 0)
    for c in from_x2:
        c.start()
    give_core0(2, 0)

    @pl.when(has_rim)
    def _():
        wait_shard(1, recv_rim, 0, 1)
        for c in rim_from_y:
            c.start()

    dense[...] = jnp.zeros_like(dense)
    for n, shift in enumerate(SHIFTS):
        for par, tap in taps_of_shift(shift):
            dense[par * 32 : (par + 1) * 32, n * 256 : (n + 1) * 256] = weight_ref[tap]

    wait_shard(0, recv_own, 1, 1)
    give_core0(1, 1)
    wait_shard(0, recv_own, 3, 1)
    give_core0(3, 1)
    wait_shard(0, recv_own, 2, 1)
    give_core0(2, 1)

    @pl.when(has_rim)
    def _():
        wait_shard(1, recv_rim, 2, 0)
        for c in rim_from_x2:
            c.start()
        for dx, dy in ((1, 0), (3, 0), (1, 1), (3, 1), (2, 1)):
            wait_shard(1, recv_rim, dx, dy)

    @pl.when(core == 0)
    def _():
        for dx in range(4):
            for dy in range(2):
                wait_shard(1, recv_rim, dx, dy)

    lane = lax.broadcasted_iota(jnp.int32, (128, Z), 1)

    def shift_z(plane, half):
        start = pl.multiple_of(half * 128, 128)
        for j in range(Y):
            block = grads[plane, 0, pl.ds(start, 128), j * Z : (j + 1) * Z].astype(F32)
            moved = pltpu.roll(block, Z - 1, 1)
            grads[plane, 1, pl.ds(start, 128), j * Z : (j + 1) * Z] = jnp.where(
                lane == Z - 1, 0.0, moved
            ).astype(BF16)

    def filter_terms(chunk, half):
        start = pl.multiple_of(half * 128, 128)
        for sx, sy, sz in SHIFTS:
            pairs = taps_of_shift((sx, sy, sz))
            maps = jnp.concatenate([acts[p * 32 : (p + 1) * 32] for p, _ in pairs], 0)
            window = grads[sx, sz, pl.ds(start, 128), sy * Z : sy * Z + CELLS]
            product = lax.dot_general(
                maps, window, (((1,), (1,)), ((), ())), preferred_element_type=F32
            )
            for n, (_, tap) in enumerate(pairs):
                terms[chunk, pl.ds(tap, 32, stride=PAD), :] = product[n * 32 : (n + 1) * 32]

    halves = [x // 2, 1 - x // 2]
    mates = []
    for chunk in range(2):
        for plane in range(2):
            shift_z(plane, halves[chunk])
        filter_terms(chunk, halves[chunk])
        theirs = pl.multiple_of((1 - core) * 512, 512)
        c = copy(
            terms.at[chunk, pl.ds(theirs, 512)], from_mate.at[chunk],
            fw_send.at[chunk], fw_recv.at[chunk], mate,
        )
        c.start()
        mates.append(c)

    ours = pl.multiple_of(core * 512, 512)
    rs_sent = []
    for chunk in range(2):
        mates[chunk].wait_recv()
        total = terms[chunk, pl.ds(ours, 512), :] + from_mate[chunk]
        rs_own[chunk] = total.reshape(16, PAD, 128)
        rs_out[chunk] = encode(total.reshape(16, PAD, 128))
        for d in range(1, 16):
            a, k = d // NZ, d % NZ
            c = copy(
                rs_out.at[chunk, peer_w(d)], rs_in.at[chunk, a * NZ + (NZ - k) % NZ],
                rs_send.at[chunk, d], rs_recv.at[chunk], peer(d),
            )
            c.start()
            rs_sent.append(c)

    def wait_many(ref, sem):
        pltpu.make_async_copy(ref, ref, sem).wait()

    def maps_gradient(tile):
        columns = []
        for sx, sy, sz in SHIFTS:
            columns.append(grads[sx, sz, :, sy * Z + tile * 256 : sy * Z + (tile + 1) * 256])
        window = jnp.concatenate(columns, 0)
        sums = jnp.dot(dense[...], window, preferred_element_type=F32)
        for j in range(2):
            rows32[pl.ds(tile * 2 + j, 256, stride=Y)] = sums[:, j * Z : (j + 1) * Z]

    for tile in range(4):
        maps_gradient(tile)

    ag_sent = []
    for chunk in range(2):
        wait_many(rs_in.at[chunk, pl.ds(1, 15)], rs_recv.at[chunk])
        total = rs_own[chunk, w]
        total = total + jnp.sum(decode(rs_in[chunk, 1:16]), axis=0)
        ag[chunk, core, w] = encode((total * norm)[None])[0]
        for d in range(1, 16):
            c = copy(
                ag.at[chunk, core, w], ag.at[chunk, core, w],
                ag_send.at[chunk, d], ag_recv.at[chunk], peer(d),
            )
            c.start()
            ag_sent.append(c)

    for tile in range(4, 8):
        maps_gradient(tile)
    for par in range(8):
        out_act[:, 0, par] = (
            rows32[par * 32 * Y : (par + 1) * 32 * Y].reshape(32, Y, Z).astype(BF16)
        )

    ag_mate = []
    for chunk in range(2):
        wait_many(ag.at[chunk, core, pl.ds(0, 15)], ag_recv.at[chunk])
        c = copy(
            ag.at[chunk, core], ag.at[chunk, core],
            fw_send.at[2 + chunk], fw_recv.at[2 + chunk], mate,
        )
        c.start()
        ag_mate.append(c)
    for chunk in range(2):
        ag_mate[chunk].wait_recv()
        final[...] = decode(ag[chunk].reshape(32, PAD, 128)).reshape(32 * PAD, 128)
        start = pl.multiple_of(halves[chunk] * 128, 128)
        for tap in range(27):
            out_w[tap, :, pl.ds(start, 128)] = final[pl.ds(tap, 32, stride=PAD)]

    for c in own + from_y + from_x2 + mates + rs_sent + ag_sent + ag_mate:
        c.wait_send()

    @pl.when(has_rim)
    def _():
        for c in rim_own + rim_from_y + rim_from_x2:
            c.wait_send()

    @pl.when(gives_rim)
    def _():
        rim_first.wait_send()

    @pl.when(core == 1)
    def _():
        for dx in range(4):
            for dy in range(2):
                to_core0(dx, dy).wait_send()


def on_device(activations, grad_out, weight):
    _, planes, _, out_y, out_z = activations.shape
    norm = 1.0 / math.sqrt(planes * out_y * out_z * lax.axis_size("grid"))
    vmem = pl.BlockSpec(memory_space=pltpu.VMEM)
    dma = pltpu.SemaphoreType.DMA
    return pl.pallas_call(
        lambda *refs: kernel(norm, *refs),
        out_shape=(
            jax.ShapeDtypeStruct(activations.shape, BF16),
            jax.ShapeDtypeStruct(weight.shape, F32),
        ),
        in_specs=[vmem] * 3,
        out_specs=(vmem, vmem),
        scratch_shapes=[
            pltpu.VMEM((256 * Y, Z), F32),
            pltpu.VMEM((256, CELLS), BF16),
            pltpu.VMEM((2, 2, 256, CELLS + Z), BF16),
            pltpu.VMEM((256, 2048), BF16),
            pltpu.VMEM((2, 32 * PAD, 128), F32),
            pltpu.VMEM((2, 16 * PAD, 128), F32),
            pltpu.VMEM((2, 16, PAD, 128), F32),
            pltpu.VMEM((2, 16, PAD, 128), BF16),
            pltpu.VMEM((2, 16, PAD, 128), BF16),
            pltpu.VMEM((2, 2, 16, PAD, 128), BF16),
            pltpu.VMEM((32 * PAD, 128), F32),
            dma((7,)), dma((8,)), dma((7,)), dma((8,)), dma((8,)), dma((8,)),
            dma((2, 16)), dma((2,)), dma((2, 16)), dma((2,)), dma((4,)), dma((4,)),
        ],
        compiler_params=pltpu.CompilerParams(
            collective_id=0, has_side_effects=True, vmem_limit_bytes=48 << 20
        ),
    )(activations, grad_out, weight)


def solution(mesh):
    placed = (
        P("chan", "grid", None, None, None),
        P("chan", "grid", None, None),
        P(None, "chan", None),
    )
    return jax.shard_map(
        on_device,
        mesh=mesh,
        in_specs=placed,
        out_specs=(P("chan", "grid", None, None, None), P(None, "chan", None)),
        check_vma=False,
    )
```

time: 419 us -> 59.2 us (0.14)
  waiting for transfers between devices: 271 us -> 0 us
  matrix products: 77 us -> 0 us
  Pallas kernels: 0 us -> 53.4 us
  local copies, waits for them, and re-layouts: 38 us -> 5.02 us
  between operations: 14.5 us -> 0.65 us
  starting transfers between devices: 12.8 us -> 0 us
    psum x1 -> x0, waiting for transfers between devices: 237 us -> none  [on_device(): grad_weight = lax.psum(grad_w, 'grid') * scale_norm]
    dot_general x54 -> x0, matrix products: 77 us -> none  [the longest x27 40.9 us: on_device(): jnp.dot(weight[tap_x * 9 + tap_y * 3 + tap_z], window, preferred_element_...]
    pallas_call x0 -> x1, Pallas kernels: none -> 53.4 us  [on_device(): pl.pallas_call(lambda *refs: kernel(norm, *refs), out_shape=(jax.ShapeDty...]
    all_gather x1 -> x0, waiting for transfers between devices: 34 us -> none  [on_device(): gathered = lax.all_gather(grad_out, 'chan', axis=0, tiled=True)]
    unnamed x72 -> x8, local copies, waits for them, and re-layouts: 25.9 us -> 5.02 us
    ppermute x2 -> x0, starting transfers between devices: 12.7 us -> none  [shifted_2(): return lax.ppermute(block, axis, route)]
    slice x9 -> x0, local copies, waits for them, and re-layouts: 6.41 us -> none  [the longest x4 4.34 us: shifted_grads(): y_shifted[:, :, :, 1:]]
  transfers between devices with their start and end apart: 4 -> 0, of which waited for: 2 -> 0; matrix products, arithmetic and copies ran while one was open for 11% -> 0% of each run, Pallas kernels for 0% -> 0%
where the time goes in v1:
time: 59.2 us; the launch traced here: 59 us
  Pallas kernels  53.4 us (90%)
  local copies, waits for them, and re-layouts  5.02 us (8%)
  between operations  0.65 us (1%)
    pallas_call x1, Pallas kernels, on_device(): pl.pallas_call(lambda *refs: kernel(norm, *refs), out_shape=(jax.ShapeDty...  53.4 us
    unnamed x8, local copies, waits for them, and re-layouts  5.02 us

profile of v1, /device:TPU:1, one launch (start us, length us, event | category | flops | bytes accessed | tf_op | source)
XLA Modules:
  0.0 59.0 jit_solution(8281688308582569646)
XLA Ops:
  0.6 0.0 copy-start
  0.6 1.2 %copy-done = bf16[32,1,8,16,128]{4,3,2,1,0:T(8,128)(2,1)S(1)} copy-done((bf16[32,1,8,16,128]{4,3,2,1,0:T(8,128)(2,1)S(1)}, bf16[32,1,8,16,128]{4,3,2,1,0:T(8,128)(2,1)}, u32[]{:S(2)}) %copy-start) | copy-done | bytes 1048600
  1.9 0.0 copy-start.1
  1.9 1.0 %copy-done.1 = bf16[27,32,256]{2,1,0:T(8,128)(2,1)S(1)} copy-done((bf16[27,32,256]{2,1,0:T(8,128)(2,1)S(1)}, bf16[27,32,256]{2,1,0:T(8,128)(2,1)}, u32[]{:S(2)}) %copy-start.1) | copy-done | bytes 442392
  2.9 0.0 copy-start.2
  2.9 0.9 %copy-done.2 = bf16[32,1,16,128]{3,2,1,0:T(8,128)(2,1)S(1)} copy-done((bf16[32,1,16,128]{3,2,1,0:T(8,128)(2,1)S(1)}, bf16[32,1,16,128]{3,2,1,0:T(8,128)(2,1)}, u32[]{:S(2)}) %copy-start.2) | copy-done | bytes 131096
  3.8 53.4 %shard_map.50 = (bf16[32,1,8,16,128]{4,3,2,1,0:T(8,128)(2,1)S(1)}, f32[27,32,256]{2,1,0:T(8,128)S(1)}) custom-call(bf16[32,1,8,16,128]{4,3,2,1,0:T(8,128)(2,1)S(1)} %copy-done, bf16[32,1,16,128]{3,2,1,0:T(8,128)(2,1)S(1)} %copy-done.2, bf16[27,32,256]{2,1,0:T(8,128)(2,1)S(1)} %copy-done.1), custom_call_target="tpu_custom_call" | custom-call | tf_op jit(solution)/shard_map/pallas_call | solution.py:362
  57.1 1.0 %copy.7 = bf16[32,1,8,16,128]{4,3,2,1,0:T(8,128)(2,1)} copy(bf16[32,1,8,16,128]{4,3,2,1,0:T(8,128)(2,1)S(1)} %get-tuple-element.4) | data formatting | bytes 2097152
  58.1 0.9 %copy.8 = f32[27,32,256]{2,1,0:T(8,128)} copy(f32[27,32,256]{2,1,0:T(8,128)S(1)} %get-tuple-element.5) | data formatting | bytes 1769472
Async XLA Ops:
  0.6 1.2 %copy-start = (bf16[32,1,8,16,128]{4,3,2,1,0:T(8,128)(2,1)S(1)}, bf16[32,1,8,16,128]{4,3,2,1,0:T(8,128)(2,1)}, u32[]{:S(2)}) copy-start(bf16[32,1,8,16,128]{4,3,2,1,0:T(8,128)(2,1)} %refs_0_.1) | copy-start | bytes 3145732
  1.9 1.0 %copy-start.1 = (bf16[27,32,256]{2,1,0:T(8,128)(2,1)S(1)}, bf16[27,32,256]{2,1,0:T(8,128)(2,1)}, u32[]{:S(2)}) copy-start(bf16[27,32,256]{2,1,0:T(8,128)(2,1)} %refs_2_.1) | copy-start | bytes 1327108
  2.9 0.9 %copy-start.2 = (bf16[32,1,16,128]{3,2,1,0:T(8,128)(2,1)S(1)}, bf16[32,1,16,128]{3,2,1,0:T(8,128)(2,1)}, u32[]{:S(2)}) copy-start(bf16[32,1,16,128]{3,2,1,0:T(8,128)(2,1)} %refs_1_.1) | copy-start | bytes 393220

commit v2 on v1

v2 whole, which is shorter than its diff:
```python
import math

import jax
import jax.numpy as jnp
from jax import lax
from jax.experimental import pallas as pl
from jax.experimental.pallas import tpu as pltpu
from jax.sharding import PartitionSpec as P

MESH = pl.DeviceIdType.MESH
F32, BF16 = jnp.float32, jnp.bfloat16
NX, NYL, NZ, NYH = 4, 2, 8, 2
Y, Z = 16, 128
CELLS = Y * Z
ROWS = 16
ODD = 128
SPAN = 240.0


def tap_of(par, step):
    if par == 0:
        return 1 if step == 0 else None
    return 2 if step == 0 else 0


def taps_of_shift(shift):
    found = []
    for par in range(8):
        bits = (par // 4, par // 2 % 2, par % 2)
        taps = [tap_of(b, s) for b, s in zip(bits, shift)]
        if None not in taps:
            found.append((par, 9 * taps[0] + 3 * taps[1] + taps[2]))
    return found


PARTS = (
    ((0, 0, (0,)), (0, 1, (0,)), (1, 1, (0,))),
    ((1, 0, (0, 1)), (0, 0, (1,)), (0, 1, (1,)), (1, 1, (1,))),
)


def part_taps(part):
    return [
        tap for sy, sz, planes in PARTS[part] for sx in planes for _, tap in taps_of_shift((sx, sy, sz))
    ]


SHIFTS = [(sx, sy, sz) for sx in range(2) for sy in range(2) for sz in range(2)]


def encode(values):
    largest = jnp.max(jnp.abs(values), axis=-2, keepdims=True)
    scale = jnp.maximum((largest * 1.01).astype(BF16).astype(F32), 1e-30)
    level = values * (SPAN / scale)
    power = jnp.exp2(jnp.abs(level) - SPAN / 2)
    power = jnp.where(values < 0, -power, power)
    row = lax.broadcasted_iota(jnp.int32, values.shape, values.ndim - 2)
    return jnp.where(row >= ROWS - 2, scale, power).astype(BF16)


def decode(codes):
    codes = codes.astype(F32)
    scale = codes[..., ROWS - 2 : ROWS - 1, :] * (1.0 / SPAN)
    level = (jnp.log2(jnp.abs(codes)) + SPAN / 2) * scale
    return jnp.where(codes < 0, -level, level)


def kernel(
    norm, act_hbm, grad_hbm, weight_hbm, out_act, ag,
    act_ref, grad_ref, weight_ref, rows32, acts, before_maps, relay, grads, dense,
    terms, from_mate, rs_own, rs_out, rs_in,
    local, send_own, recv_own, send_rim, recv_rim, hop_send, hop_recv,
    rs_send, rs_recv, ag_send, ag_recv, fw_send, fw_recv,
):
    g, chan = lax.axis_index("grid"), lax.axis_index("chan")
    w, core = g >> 1, g & 1
    x, yl = chan >> 1, chan & 1
    last = 2 * NZ * NYH - 1

    def chan_of(dx, dy):
        return ((x + dx) & (NX - 1)) * NYL + (yl ^ dy)

    def at_chan(dx, dy):
        return (g, chan_of(dx, dy))

    mate = (g + 1 - 2 * core, chan)
    before = (jnp.maximum(g - 1, 0), chan)
    following = (jnp.minimum(g + 1, last), chan)

    def peer_w(d):
        return ((w & NZ) ^ (d & NZ)) + ((w + d) & (NZ - 1))

    def slot_of(d):
        return (d & NZ) + ((NZ - d) & (NZ - 1))

    def peer(d):
        return (peer_w(d) * 2 + core, chan)

    has_rim = jnp.logical_and(core == 1, g < last)
    gives_rim = jnp.logical_and(core == 0, g > 0)

    barrier = pltpu.get_barrier_semaphore()
    near = [at_chan(1, 0), at_chan(3, 0), at_chan(0, 1), at_chan(1, 1), at_chan(3, 1), mate]
    chips = NZ * NYH
    for device in near:
        pl.semaphore_signal(barrier, inc=1, device_id=device, device_id_type=MESH)

    @pl.loop(1, chips)
    def _(d):
        pl.semaphore_signal(barrier, inc=1, device_id=peer(d), device_id_type=MESH)

    @pl.when(gives_rim)
    def _():
        pl.semaphore_signal(barrier, inc=1, device_id=before, device_id_type=MESH)

    @pl.when(has_rim)
    def _():
        pl.semaphore_signal(barrier, inc=1, device_id=following, device_id_type=MESH)

    @pl.when(g == 0)
    def _():
        pl.semaphore_signal(barrier, inc=1, device_id=(2 * NZ - 1, chan), device_id_type=MESH)

    @pl.when(g == 2 * NZ - 1)
    def _():
        pl.semaphore_signal(barrier, inc=1, device_id=(0, chan), device_id_type=MESH)

    loads = [
        pltpu.make_async_copy(grad_hbm, grad_ref, local.at[0]),
        pltpu.make_async_copy(act_hbm, act_ref, local.at[1]),
        pltpu.make_async_copy(weight_hbm, weight_ref, local.at[2]),
    ]
    for c in loads:
        c.start()

    def piece(plane, dx, dy, h):
        start = pl.multiple_of(chan_of(dx, dy) * 32 + 16 * h, 16)
        return grads.at[plane, 0, pl.ds(start, 16), pl.ds(0, CELLS)]

    loads[0].wait()
    rows32[0 : 32 * Y] = grad_ref[:, 0].astype(F32).reshape(32 * Y, Z)
    start_own = pl.multiple_of(chan * 32, 32)

    def along(j, size=Z):
        return pl.ds(pl.multiple_of(j * size, size), size)

    @pl.loop(0, Y)
    def _(j):
        grads[0, 0, pl.ds(start_own, 32), along(j)] = rows32[pl.ds(j, 32, stride=Y)].astype(BF16)

    rim_partners = jnp.logical_or(gives_rim, has_rim).astype(jnp.int32)
    rim_partners += jnp.logical_or(g == 0, g == 2 * NZ - 1).astype(jnp.int32)
    pl.semaphore_wait(barrier, len(near) + chips - 1 + rim_partners)

    def copy(src, dst, send, recv, device):
        return pltpu.make_async_remote_copy(
            src_ref=src, dst_ref=dst, send_sem=send, recv_sem=recv,
            device_id=device, device_id_type=MESH,
        )

    def gather_copies(plane, send, recv):
        count = [0]

        def one(dx, dy, h, slot, device):
            n = count[0]
            count[0] += 1
            ref = piece(plane, dx, dy, h)
            return copy(ref, ref, send.at[n], recv.at[slot, h], device)

        own = []
        for h in range(2):
            own.append(one(0, 0, h, 1, at_chan(0, 1)))
            own.append(one(0, 0, h, 6, at_chan(1, 0)))
            own.append(one(0, 0, h, 2, at_chan(3, 0)))
        passed = []
        for h in range(2):
            passed.append(
                ((0, 1, h), [one(0, 1, h, 7, at_chan(1, 0)), one(0, 1, h, 3, at_chan(3, 0))])
            )
            dx = 3 - 2 * h
            passed.append(
                (
                    (dx, 0, h),
                    [one(dx, 0, h, 4, at_chan(4 - dx, 0)), one(dx, 0, h, 5, at_chan(4 - dx, 1))],
                )
            )
        return own, passed

    def wait_piece(plane, recv, slot, h):
        ref = piece(plane, 0, 0, h)
        pltpu.make_async_copy(ref, ref, recv.at[slot, h]).wait()

    own, passed = gather_copies(0, send_own, recv_own)
    rim_own, rim_passed = gather_copies(1, send_rim, recv_rim)
    rim_first = [
        copy(
            piece(0, 0, 0, h), piece(1, 0, 0, h), hop_send.at[h], recv_rim.at[0, h], before
        )
        for h in range(2)
    ]
    half_odd = ODD // 2
    crosses, relays = g == 2 * NZ - 1, g == 0
    relay_at = (0, chan)
    upper = acts.at[pl.ds(ODD + half_odd, half_odd)]
    arrives = before_maps.at[pl.ds(half_odd, half_odd)]
    odd_lower = copy(
        acts.at[pl.ds(ODD, half_odd)], before_maps.at[pl.ds(0, half_odd)],
        hop_send.at[2], hop_recv.at[0], following,
    )
    odd_upper = copy(upper, arrives, hop_send.at[4], hop_recv.at[2], following)
    odd_to_relay = copy(upper, relay, hop_send.at[4], hop_recv.at[3], relay_at)
    odd_relayed = copy(relay, arrives, hop_send.at[5], hop_recv.at[2], (2 * NZ, chan))
    plane_cells = pl.ds(0, CELLS)
    whole_plane = copy(
        grads.at[0, 0, :, plane_cells], grads.at[1, 0, :, plane_cells],
        hop_send.at[3], hop_recv.at[1], mate,
    )

    for c in own:
        c.start()

    loads[1].wait()

    @pl.loop(0, 8)
    def _(par):
        rows32[along(par, 32 * Y)] = act_ref[:, 0, par].astype(F32).reshape(32 * Y, Z)

    for base in (ODD, 0):

        @pl.loop(0, Y)
        def _(j):
            acts[base : base + ODD, along(j)] = rows32[
                pl.ds(base * Y + j, ODD, stride=Y)
            ].astype(BF16)

        if base:

            @pl.when(g < last)
            def _():
                odd_lower.start()

            @pl.when(jnp.logical_and(g < last, jnp.logical_not(crosses)))
            def _():
                odd_upper.start()

            @pl.when(crosses)
            def _():
                odd_to_relay.start()

    @pl.when(gives_rim)
    def _():
        for c in rim_first:
            c.start()

    for plane in range(2):
        for sz in range(2):
            grads[plane, sz, :, CELLS:] = jnp.zeros((256, Z), BF16)

    @pl.when(g == last)
    def _():
        grads[1, 0, :, 0:CELLS] = jnp.zeros((256, CELLS), BF16)

    @pl.when(g == 0)
    def _():
        before_maps[...] = jnp.zeros_like(before_maps)

    terms[...] = jnp.zeros_like(terms)

    def pass_on(plane, recv, steps):
        for (dx, dy, h), copies in steps:
            wait_piece(plane, recv, dx * 2 + dy, h)
            for c in copies:
                c.start()

    pass_on(0, recv_own, passed)

    @pl.when(relays)
    def _():
        odd_to_relay.wait_recv()
        odd_relayed.start()


    loads[2].wait()
    dense[...] = jnp.zeros_like(dense)
    for n, shift in enumerate(SHIFTS):
        for par, tap in taps_of_shift(shift):
            dense[par * 32 : (par + 1) * 32, n * 256 : (n + 1) * 256] = weight_ref[tap]

    lane = lax.broadcasted_iota(jnp.int32, (128, Z), 1)

    def shift_z(plane, half):
        start = pl.multiple_of(half * 128, 128)

        @pl.loop(0, Y)
        def _(j):
            block = grads[plane, 0, pl.ds(start, 128), along(j)].astype(F32)
            moved = pltpu.roll(block, Z - 1, 1)
            grads[plane, 1, pl.ds(start, 128), along(j)] = jnp.where(
                lane == Z - 1, 0.0, moved
            ).astype(BF16)

    def filter_terms(part):
        row = 0
        for sy, sz, planes in PARTS[part]:
            maps = []
            for sx in planes:
                for par, _ in taps_of_shift((sx, sy, sz)):
                    source, base = (before_maps, 4) if sx else (acts, 0)
                    maps.append(source[(par - base) * 32 : (par - base + 1) * 32])
            window = grads[0, sz, :, sy * Z : sy * Z + CELLS]
            product = lax.dot_general(
                jnp.concatenate(maps, 0), window, (((1,), (1,)), ((), ())),
                preferred_element_type=F32,
            )
            for n in range(len(maps)):
                for half in range(2):
                    terms[part, half, pl.ds(row, 32, stride=ROWS), :] = product[
                        n * 32 : (n + 1) * 32, half * 128 : (half + 1) * 128
                    ]
                row += 1

    mine = 16 * ROWS
    theirs = pl.multiple_of((1 - core) * mine, mine)
    ours = pl.multiple_of(core * mine, mine)
    to_mate = [
        copy(
            terms.at[part, :, pl.ds(theirs, mine)], from_mate.at[part],
            fw_send.at[part], fw_recv.at[part], mate,
        )
        for part in range(2)
    ]
    halves = [x // 2, 1 - x // 2]
    near_x = 1 + 2 * lax.rem(x, 2)
    far_x = 4 - near_x

    wait_piece(0, recv_own, 6, 1)
    wait_piece(0, recv_own, 2, 0)
    for h in range(2):
        wait_piece(0, recv_own, near_x * 2 + 1, h)
    shift_z(0, halves[0])
    for slot in (4, 5):
        for h in range(2):
            wait_piece(0, recv_own, slot, h)
    for h in range(2):
        wait_piece(0, recv_own, far_x * 2 + 1, h)
    shift_z(0, halves[1])
    filter_terms(0)
    to_mate[0].start()

    @pl.when(has_rim)
    def _():
        for h in range(2):
            wait_piece(1, recv_rim, 0, h)
        for c in rim_own:
            c.start()

    @pl.when(core == 1)
    def _():
        whole_plane.start()

    def scatter(part):
        to_mate[part].wait_recv()
        for half in range(2):
            total = terms[part, half, pl.ds(ours, mine), :] + from_mate[part, half]
            total = total.reshape(16, ROWS, 128)
            rs_own[part, :, half] = total
            rs_out[part, :, half] = encode(total)

        @pl.loop(1, chips)
        def _(d):
            copy(
                rs_out.at[part, peer_w(d)], rs_in.at[part, slot_of(d)],
                rs_send.at[part], rs_recv.at[part], peer(d),
            ).start()

    def wait_many(ref, sem):
        pltpu.make_async_copy(ref, ref, sem).wait()

    scatter(0)

    @pl.when(g > 0)
    def _():
        odd_lower.wait_recv()
        odd_upper.wait_recv()

    filter_terms(1)
    to_mate[1].start()
    scatter(1)

    @pl.when(has_rim)
    def _():
        pass_on(1, recv_rim, rim_passed)

    def share(part):
        wait_many(rs_in.at[part, pl.ds(1, 15)], rs_recv.at[part])
        total = rs_own[part, w] + jnp.sum(decode(rs_in[part, 1:16]), axis=0)
        ag[part, core, w] = encode(total * norm)

        @pl.loop(1, chips)
        def _(d):
            block = ag.at[part, core, w]
            copy(block, block, ag_send.at[part], ag_recv.at[part], peer(d)).start()

    share(0)
    share(1)

    @pl.when(has_rim)
    def _():
        for slot, h in ((6, 1), (2, 0)):
            wait_piece(1, recv_rim, slot, h)
        for slot in (3, 4, 5, 7):
            for h in range(2):
                wait_piece(1, recv_rim, slot, h)

    @pl.when(core == 0)
    def _():
        whole_plane.wait_recv()

    for half in range(2):
        shift_z(1, half)

    @pl.loop(0, CELLS // 256)
    def _(tile):
        columns = []
        for sx, sy, sz in SHIFTS:
            cells = pl.ds(pl.multiple_of(tile * 256 + sy * Z, Z), 256)
            columns.append(grads[sx, sz, :, cells])
        window = jnp.concatenate(columns, 0)
        sums = jnp.dot(dense[...], window, preferred_element_type=F32)
        for j in range(2):
            rows32[pl.ds(tile * 2 + j, 256, stride=Y)] = sums[:, j * Z : (j + 1) * Z]

    @pl.loop(0, 8)
    def _(par):
        out_act[:, 0, par] = rows32[along(par, 32 * Y)].reshape(32, Y, Z).astype(BF16)

    ag_mate = []
    for part in range(2):
        wait_many(ag.at[part, core, pl.ds(0, 15)], ag_recv.at[part])
        c = copy(
            ag.at[part, core], ag.at[part, core],
            fw_send.at[2 + part], fw_recv.at[2 + part], mate,
        )
        c.start()
        ag_mate.append(c)
    for c in ag_mate:
        c.wait_recv()

    sent = own + [c for _, copies in passed for c in copies]
    for c in sent + to_mate + ag_mate:
        c.wait_send()
    for part in range(2):
        wait_many(rs_out.at[part, pl.ds(1, 15)], rs_send.at[part])
        wait_many(ag.at[part, core, pl.ds(1, 15)], ag_send.at[part])

    @pl.when(has_rim)
    def _():
        for c in rim_own + [c for _, copies in rim_passed for c in copies]:
            c.wait_send()

    @pl.when(gives_rim)
    def _():
        for c in rim_first:
            c.wait_send()

    @pl.when(g < last)
    def _():
        odd_lower.wait_send()
        odd_upper.wait_send()

    @pl.when(relays)
    def _():
        odd_relayed.wait_send()

    @pl.when(core == 1)
    def _():
        whole_plane.wait_send()


def finish(codes, act_ref, out_act, out_w, terms, result, sems):
    moved = pltpu.make_async_copy(act_ref, out_act, sems.at[0])
    moved.start()
    for part in range(2):
        terms[part] = decode(codes[part]).reshape(32 * 2 * ROWS, 128)
        for row, tap in enumerate(part_taps(part)):
            for half in range(2):
                result[tap, :, half * 128 : (half + 1) * 128] = terms[
                    part, pl.ds(half * ROWS + row, 32, stride=2 * ROWS)
                ]
    written = pltpu.make_async_copy(result, out_w, sems.at[1])
    written.start()
    moved.wait()
    written.wait()


def on_device(activations, grad_out, weight):
    _, planes, _, out_y, out_z = activations.shape
    norm = 1.0 / math.sqrt(planes * out_y * out_z * lax.axis_size("grid"))
    vmem = pl.BlockSpec(memory_space=pltpu.VMEM)
    anywhere = pl.BlockSpec(memory_space=pl.ANY)
    dma = pltpu.SemaphoreType.DMA
    maps = jax.ShapeDtypeStruct(activations.shape, BF16)
    code_shape = (2, 2, 16, 2, ROWS, 128)
    grad_act, codes = pl.pallas_call(
        lambda *refs: kernel(norm, *refs),
        out_shape=(maps, jax.ShapeDtypeStruct(code_shape, BF16)),
        in_specs=[pl.BlockSpec(memory_space=pltpu.HBM)] * 3,
        out_specs=(vmem, vmem),
        scratch_shapes=[
            pltpu.VMEM(activations.shape, BF16),
            pltpu.VMEM(grad_out.shape, BF16),
            pltpu.VMEM(weight.shape, BF16),
            pltpu.VMEM((256 * Y, Z), F32),
            pltpu.VMEM((256, CELLS), BF16),
            pltpu.VMEM((ODD, CELLS), BF16),
            pltpu.VMEM((ODD // 2, CELLS), BF16),
            pltpu.VMEM((2, 2, 256, CELLS + Z), BF16),
            pltpu.VMEM((256, 2048), BF16),
            pltpu.VMEM((2, 2, 32 * ROWS, 128), F32),
            pltpu.VMEM((2, 2, 16 * ROWS, 128), F32),
            pltpu.VMEM((2, 16, 2, ROWS, 128), F32),
            pltpu.VMEM((2, 16, 2, ROWS, 128), BF16),
            pltpu.VMEM((2, 16, 2, ROWS, 128), BF16),
            dma((3,)), dma((14,)), dma((8, 2)), dma((14,)), dma((8, 2)), dma((6,)), dma((4,)),
            dma((2,)), dma((2,)), dma((2,)), dma((2,)), dma((4,)), dma((4,)),
        ],
        compiler_params=pltpu.CompilerParams(
            collective_id=0, has_side_effects=True, vmem_limit_bytes=48 << 20
        ),
    )(*(pltpu.with_memory_space_constraint(v, pltpu.HBM) for v in (activations, grad_out, weight)))
    return pl.pallas_call(
        finish,
        out_shape=(maps, jax.ShapeDtypeStruct(weight.shape, F32)),
        in_specs=[vmem, vmem],
        out_specs=(anywhere, anywhere),
        scratch_shapes=[
            pltpu.VMEM((2, 32 * 2 * ROWS, 128), F32),
            pltpu.VMEM(weight.shape, F32),
            dma((2,)),
        ],
        compiler_params=pltpu.CompilerParams(vmem_limit_bytes=16 << 20),
    )(codes, grad_act)


def solution(mesh):
    placed = (
        P("chan", "grid", None, None, None),
        P("chan", "grid", None, None),
        P(None, "chan", None),
    )
    return jax.shard_map(
        on_device,
        mesh=mesh,
        in_specs=placed,
        out_specs=(P("chan", "grid", None, None, None), P(None, "chan", None)),
        check_vma=False,
    )
```

time: 59.2 us -> 52.3 us (0.88)
  local copies, waits for them, and re-layouts: 5.02 us -> 0 us
  Pallas kernels: 53.4 us -> 51.5 us
    unnamed x8 -> x0, local copies, waits for them, and re-layouts: 5.02 us -> none
    pallas_call x1 -> x2, Pallas kernels: 53.4 us -> 51.5 us  [the longest x1 49.6 us: on_device(): pl.pallas_call(lambda *refs: kernel(norm, *refs), out_shape=(maps, jax.Sh...]
where the time goes in v2:
time: 52.3 us; the launch traced here: 52.2 us
  Pallas kernels  51.5 us (98%)
  between operations  0.64 us (1%)
    pallas_call x1, Pallas kernels, on_device(): pl.pallas_call(lambda *refs: kernel(norm, *refs), out_shape=(maps, jax.Sh...  49.6 us
    pallas_call x1, Pallas kernels, on_device(): pl.pallas_call(finish, out_shape=(maps, jax.ShapeDtypeStruct(weight.shape...  1.9 us

profile of v2, /device:TPU:1, one launch (start us, length us, event | category | flops | bytes accessed | tf_op | source)
XLA Modules:
  0.0 52.2 jit_solution(3735090375687355740)
XLA Ops:
  0.6 49.6 %shard_map.50 = (bf16[32,1,8,16,128]{4,3,2,1,0:T(8,128)(2,1)S(1)}, bf16[2,2,16,2,16,128]{5,4,3,2,1,0:T(8,128)(2,1)S(1)}) custom-call(bf16[32,1,8,16,128]{4,3,2,1,0:T(8,128)(2,1)} %refs_0_.1, bf16[32,1,16,128]{3,2,1,0:T(8,128)(2,1)} %refs_1_.1, bf16[27,32,256]{2,1,0:T(8,128)(2,1)} %refs_2_.1), custom_call_target="tpu_custom_call" | custom-call | tf_op jit(solution)/shard_map/pallas_call | solution.py:504
  50.3 1.9 %shard_map.51 = (bf16[32,1,8,16,128]{4,3,2,1,0:T(8,128)(2,1)}, f32[27,32,256]{2,1,0:T(8,128)}) custom-call(bf16[2,2,16,2,16,128]{5,4,3,2,1,0:T(8,128)(2,1)S(1)} %get-tuple-element.4.codes, bf16[32,1,8,16,128]{4,3,2,1,0:T(8,128)(2,1)S(1)} %get-tuple-element.5.act_ref), custom_call_target="tpu_custom_call" | custom-call | tf_op jit(solution)/shard_map/pallas_call | solution.py:531

commit v3 on v2

--- a/solution.py
+++ b/solution.py
@@ -70,7 +70,7 @@
     act_ref, grad_ref, weight_ref, rows32, acts, before_maps, relay, grads, dense,
     terms, from_mate, rs_own, rs_out, rs_in,
     local, send_own, recv_own, send_rim, recv_rim, hop_send, hop_recv,
-    rs_send, rs_recv, ag_send, ag_recv, fw_send, fw_recv,
+    rs_send, rs_recv, ag_send, ag_recv, fw_send, fw_recv, greeted,
 ):
     g, chan = lax.axis_index("grid"), lax.axis_index("chan")
     w, core = g >> 1, g & 1
@@ -102,12 +102,10 @@
     barrier = pltpu.get_barrier_semaphore()
     near = [at_chan(1, 0), at_chan(3, 0), at_chan(0, 1), at_chan(1, 1), at_chan(3, 1), mate]
     chips = NZ * NYH
+    next_z, before_z, other_y = peer(1), peer(NZ - 1), peer(NZ)
+    near += [next_z, before_z, other_y]
     for device in near:
         pl.semaphore_signal(barrier, inc=1, device_id=device, device_id_type=MESH)
-
-    @pl.loop(1, chips)
-    def _(d):
-        pl.semaphore_signal(barrier, inc=1, device_id=peer(d), device_id_type=MESH)
 
     @pl.when(gives_rim)
     def _():
@@ -150,7 +148,7 @@
 
     rim_partners = jnp.logical_or(gives_rim, has_rim).astype(jnp.int32)
     rim_partners += jnp.logical_or(g == 0, g == 2 * NZ - 1).astype(jnp.int32)
-    pl.semaphore_wait(barrier, len(near) + chips - 1 + rim_partners)
+    pl.semaphore_wait(barrier, len(near) + rim_partners)
 
     def copy(src, dst, send, recv, device):
         return pltpu.make_async_remote_copy(
@@ -216,8 +214,13 @@
         hop_send.at[3], hop_recv.at[1], mate,
     )
 
+    def greet(turn, *devices):
+        for device in devices:
+            pl.semaphore_signal(greeted.at[turn], inc=1, device_id=device, device_id_type=MESH)
+
     for c in own:
         c.start()
+    greet(0, next_z, before_z)
 
     loads[1].wait()
 
@@ -272,7 +275,11 @@
             for c in copies:
                 c.start()
 
+    pl.semaphore_wait(greeted.at[0], 2)
+    greet(1, peer(2), peer(NZ - 2))
     pass_on(0, recv_own, passed)
+    pl.semaphore_wait(greeted.at[1], 2)
+    greet(2, other_y)
 
     @pl.when(relays)
     def _():
@@ -376,6 +383,7 @@
     def wait_many(ref, sem):
         pltpu.make_async_copy(ref, ref, sem).wait()
 
+    pl.semaphore_wait(greeted.at[2], 1)
     scatter(0)
 
     @pl.when(g > 0)
@@ -523,6 +531,7 @@
             pltpu.VMEM((2, 16, 2, ROWS, 128), BF16),
             dma((3,)), dma((14,)), dma((8, 2)), dma((14,)), dma((8, 2)), dma((6,)), dma((4,)),
             dma((2,)), dma((2,)), dma((2,)), dma((2,)), dma((4,)), dma((4,)),
+            pltpu.SemaphoreType.REGULAR((3,)),
         ],
         compiler_params=pltpu.CompilerParams(
             collective_id=0, has_side_effects=True, vmem_limit_bytes=48 << 20

time: 52.3 us -> 47.3 us (0.904)
  Pallas kernels: 51.5 us -> 46.6 us
    pallas_call x1, Pallas kernels: 49.6 us -> 44.7 us  [on_device(): pl.pallas_call(lambda *refs: kernel(norm, *refs), out_shape=(maps, jax.Sh...]
where the time goes in v3:
time: 47.3 us; the launch traced here: 47.2 us
  Pallas kernels  46.6 us (99%)
  between operations  0.64 us (1%)
    pallas_call x1, Pallas kernels, on_device(): pl.pallas_call(lambda *refs: kernel(norm, *refs), out_shape=(maps, jax.Sh...  44.7 us
    pallas_call x1, Pallas kernels, on_device(): pl.pallas_call(finish, out_shape=(maps, jax.ShapeDtypeStruct(weight.shape...  1.9 us

profile of v3, /device:TPU:1, one launch (start us, length us, event | category | flops | bytes accessed | tf_op | source)
XLA Modules:
  0.0 47.2 jit_solution(2832967894741441138)
XLA Ops:
  0.6 44.7 %shard_map.50 = (bf16[32,1,8,16,128]{4,3,2,1,0:T(8,128)(2,1)S(1)}, bf16[2,2,16,2,16,128]{5,4,3,2,1,0:T(8,128)(2,1)S(1)}) custom-call(bf16[32,1,8,16,128]{4,3,2,1,0:T(8,128)(2,1)} %refs_0_.1, bf16[32,1,16,128]{3,2,1,0:T(8,128)(2,1)} %refs_1_.1, bf16[27,32,256]{2,1,0:T(8,128)(2,1)} %refs_2_.1), custom_call_target="tpu_custom_call" | custom-call | tf_op jit(solution)/shard_map/pallas_call | solution.py:512
  45.3 1.9 %shard_map.51 = (bf16[32,1,8,16,128]{4,3,2,1,0:T(8,128)(2,1)}, f32[27,32,256]{2,1,0:T(8,128)}) custom-call(bf16[2,2,16,2,16,128]{5,4,3,2,1,0:T(8,128)(2,1)S(1)} %get-tuple-element.4.codes, bf16[32,1,8,16,128]{4,3,2,1,0:T(8,128)(2,1)S(1)} %get-tuple-element.5.act_ref), custom_call_target="tpu_custom_call" | custom-call | tf_op jit(solution)/shard_map/pallas_call | solution.py:540

commit v4 on v3

--- a/solution.py
+++ b/solution.py
@@ -101,7 +101,7 @@
 
     barrier = pltpu.get_barrier_semaphore()
     near = [at_chan(1, 0), at_chan(3, 0), at_chan(0, 1), at_chan(1, 1), at_chan(3, 1), mate]
-    chips = NZ * NYH
+    far_first = [d for k in (4, 3, 5, 2, 6, 1, 7, 0) for d in (k + NZ, k) if d]
     next_z, before_z, other_y = peer(1), peer(NZ - 1), peer(NZ)
     near += [next_z, before_z, other_y]
     for device in near:
@@ -373,8 +373,7 @@
             rs_own[part, :, half] = total
             rs_out[part, :, half] = encode(total)
 
-        @pl.loop(1, chips)
-        def _(d):
+        for d in far_first:
             copy(
                 rs_out.at[part, peer_w(d)], rs_in.at[part, slot_of(d)],
                 rs_send.at[part], rs_recv.at[part], peer(d),
@@ -404,8 +403,7 @@
         total = rs_own[part, w] + jnp.sum(decode(rs_in[part, 1:16]), axis=0)
         ag[part, core, w] = encode(total * norm)
 
-        @pl.loop(1, chips)
-        def _(d):
+        for d in far_first:
             block = ag.at[part, core, w]
             copy(block, block, ag_send.at[part], ag_recv.at[part], peer(d)).start()
 

time: 47.3 us -> 45.7 us (0.966)
  Pallas kernels: 46.6 us -> 45 us
    pallas_call x1, Pallas kernels: 44.7 us -> 43 us  [on_device(): pl.pallas_call(lambda *refs: kernel(norm, *refs), out_shape=(maps, jax.Sh...]
where the time goes in v4:
time: 45.7 us; the launch traced here: 45.6 us
  Pallas kernels  45 us (98%)
  between operations  0.64 us (1%)
    pallas_call x1, Pallas kernels, on_device(): pl.pallas_call(lambda *refs: kernel(norm, *refs), out_shape=(maps, jax.Sh...  43 us
    pallas_call x1, Pallas kernels, on_device(): pl.pallas_call(finish, out_shape=(maps, jax.ShapeDtypeStruct(weight.shape...  1.9 us

profile of v4, /device:TPU:1, one launch (start us, length us, event | category | flops | bytes accessed | tf_op | source)
XLA Modules:
  0.0 45.6 jit_solution(722541401531399661)
XLA Ops:
  0.6 43.0 %shard_map.50 = (bf16[32,1,8,16,128]{4,3,2,1,0:T(8,128)(2,1)S(1)}, bf16[2,2,16,2,16,128]{5,4,3,2,1,0:T(8,128)(2,1)S(1)}) custom-call(bf16[32,1,8,16,128]{4,3,2,1,0:T(8,128)(2,1)} %refs_0_.1, bf16[32,1,16,128]{3,2,1,0:T(8,128)(2,1)} %refs_1_.1, bf16[27,32,256]{2,1,0:T(8,128)(2,1)} %refs_2_.1), custom_call_target="tpu_custom_call" | custom-call | tf_op jit(solution)/shard_map/pallas_call | solution.py:510
  43.7 1.9 %shard_map.51 = (bf16[32,1,8,16,128]{4,3,2,1,0:T(8,128)(2,1)}, f32[27,32,256]{2,1,0:T(8,128)}) custom-call(bf16[2,2,16,2,16,128]{5,4,3,2,1,0:T(8,128)(2,1)S(1)} %get-tuple-element.4.codes, bf16[32,1,8,16,128]{4,3,2,1,0:T(8,128)(2,1)S(1)} %get-tuple-element.5.act_ref), custom_call_target="tpu_custom_call" | custom-call | tf_op jit(solution)/shard_map/pallas_call | solution.py:538

commit v5 on v4

--- a/solution.py
+++ b/solution.py
@@ -101,7 +101,7 @@
 
     barrier = pltpu.get_barrier_semaphore()
     near = [at_chan(1, 0), at_chan(3, 0), at_chan(0, 1), at_chan(1, 1), at_chan(3, 1), mate]
-    far_first = [d for k in (4, 3, 5, 2, 6, 1, 7, 0) for d in (k + NZ, k) if d]
+    far_first = [d for high in (NZ, 0) for k in (4, 3, 5, 2, 6, 1, 7, 0) for d in (k + high,) if d]
     next_z, before_z, other_y = peer(1), peer(NZ - 1), peer(NZ)
     near += [next_z, before_z, other_y]
     for device in near:
@@ -486,17 +486,22 @@
 def finish(codes, act_ref, out_act, out_w, terms, result, sems):
     moved = pltpu.make_async_copy(act_ref, out_act, sems.at[0])
     moved.start()
-    for part in range(2):
-        terms[part] = decode(codes[part]).reshape(32 * 2 * ROWS, 128)
-        for row, tap in enumerate(part_taps(part)):
-            for half in range(2):
-                result[tap, :, half * 128 : (half + 1) * 128] = terms[
-                    part, pl.ds(half * ROWS + row, 32, stride=2 * ROWS)
-                ]
-    written = pltpu.make_async_copy(result, out_w, sems.at[1])
-    written.start()
+    span, written = 16 * 2 * ROWS, []
+    for core in range(2):
+        for part in range(2):
+            terms[part] = decode(codes[part, core]).reshape(span, 128)
+            for row, tap in enumerate(part_taps(part)):
+                for half in range(2):
+                    result[tap, core * 16 : (core + 1) * 16, half * 128 : (half + 1) * 128] = (
+                        terms[part, pl.ds(half * ROWS + row, 16, stride=2 * ROWS)]
+                    )
+        rows = pl.ds(core * 16, 16)
+        c = pltpu.make_async_copy(result.at[:, rows], out_w.at[:, rows], sems.at[1 + core])
+        c.start()
+        written.append(c)
     moved.wait()
-    written.wait()
+    for c in written:
+        c.wait()
 
 
 def on_device(activations, grad_out, weight):
@@ -541,9 +546,9 @@
         in_specs=[vmem, vmem],
         out_specs=(anywhere, anywhere),
         scratch_shapes=[
-            pltpu.VMEM((2, 32 * 2 * ROWS, 128), F32),
+            pltpu.VMEM((2, 16 * 2 * ROWS, 128), F32),
             pltpu.VMEM(weight.shape, F32),
-            dma((2,)),
+            dma((3,)),
         ],
         compiler_params=pltpu.CompilerParams(vmem_limit_bytes=16 << 20),
     )(codes, grad_act)

time: 45.7 us -> 45.2 us (0.989)
  Pallas kernels: 45 us -> 44.5 us
where the time goes in v5:
time: 45.2 us; the launch traced here: 45.1 us
  Pallas kernels  44.5 us (98%)
  between operations  0.64 us (1%)
    pallas_call x1, Pallas kernels, on_device(): pl.pallas_call(lambda *refs: kernel(norm, *refs), out_shape=(maps, jax.Sh...  42.8 us
    pallas_call x1, Pallas kernels, on_device(): pl.pallas_call(finish, out_shape=(maps, jax.ShapeDtypeStruct(weight.shape...  1.7 us

profile of v5, /device:TPU:1, one launch (start us, length us, event | category | flops | bytes accessed | tf_op | source)
XLA Modules:
  0.0 45.1 jit_solution(12416039180492360571)
XLA Ops:
  0.6 42.8 %shard_map.50 = (bf16[32,1,8,16,128]{4,3,2,1,0:T(8,128)(2,1)S(1)}, bf16[2,2,16,2,16,128]{5,4,3,2,1,0:T(8,128)(2,1)S(1)}) custom-call(bf16[32,1,8,16,128]{4,3,2,1,0:T(8,128)(2,1)} %refs_0_.1, bf16[32,1,16,128]{3,2,1,0:T(8,128)(2,1)} %refs_1_.1, bf16[27,32,256]{2,1,0:T(8,128)(2,1)} %refs_2_.1), custom_call_target="tpu_custom_call" | custom-call | tf_op jit(solution)/shard_map/pallas_call | solution.py:515
  43.4 1.7 %shard_map.51 = (bf16[32,1,8,16,128]{4,3,2,1,0:T(8,128)(2,1)}, f32[27,32,256]{2,1,0:T(8,128)}) custom-call(bf16[2,2,16,2,16,128]{5,4,3,2,1,0:T(8,128)(2,1)S(1)} %get-tuple-element.4.codes, bf16[32,1,8,16,128]{4,3,2,1,0:T(8,128)(2,1)S(1)} %get-tuple-element.5.act_ref), custom_call_target="tpu_custom_call" | custom-call | tf_op jit(solution)/shard_map/pallas_call | solution.py:543

commit v6 on v5

--- a/solution.py
+++ b/solution.py
@@ -270,10 +270,16 @@
     terms[...] = jnp.zeros_like(terms)
 
     def pass_on(plane, recv, steps):
+        turning = []
         for (dx, dy, h), copies in steps:
             wait_piece(plane, recv, dx * 2 + dy, h)
-            for c in copies:
-                c.start()
+            copies[0].start()
+            if dx:
+                turning.append(copies[1])
+            else:
+                copies[1].start()
+        for c in turning:
+            c.start()
 
     pl.semaphore_wait(greeted.at[0], 2)
     greet(1, peer(2), peer(NZ - 2))

time: 45.2 us -> 45.5 us (level)
  no operation moved by 1% of the time
where the time goes in v6:
time: 45.5 us; the launch traced here: 45.4 us
  Pallas kernels  44.7 us (98%)
  between operations  0.64 us (1%)
    pallas_call x1, Pallas kernels, on_device(): pl.pallas_call(lambda *refs: kernel(norm, *refs), out_shape=(maps, jax.Sh...  43 us
    pallas_call x1, Pallas kernels, on_device(): pl.pallas_call(finish, out_shape=(maps, jax.ShapeDtypeStruct(weight.shape...  1.7 us

profile of v6, /device:TPU:1, one launch (start us, length us, event | category | flops | bytes accessed | tf_op | source)
XLA Modules:
  0.0 45.4 jit_solution(7956754551438744039)
XLA Ops:
  0.6 43.0 %shard_map.50 = (bf16[32,1,8,16,128]{4,3,2,1,0:T(8,128)(2,1)S(1)}, bf16[2,2,16,2,16,128]{5,4,3,2,1,0:T(8,128)(2,1)S(1)}) custom-call(bf16[32,1,8,16,128]{4,3,2,1,0:T(8,128)(2,1)} %refs_0_.1, bf16[32,1,16,128]{3,2,1,0:T(8,128)(2,1)} %refs_1_.1, bf16[27,32,256]{2,1,0:T(8,128)(2,1)} %refs_2_.1), custom_call_target="tpu_custom_call" | custom-call | tf_op jit(solution)/shard_map/pallas_call | solution.py:521
  43.7 1.7 %shard_map.51 = (bf16[32,1,8,16,128]{4,3,2,1,0:T(8,128)(2,1)}, f32[27,32,256]{2,1,0:T(8,128)}) custom-call(bf16[2,2,16,2,16,128]{5,4,3,2,1,0:T(8,128)(2,1)S(1)} %get-tuple-element.4.codes, bf16[32,1,8,16,128]{4,3,2,1,0:T(8,128)(2,1)S(1)} %get-tuple-element.5.act_ref), custom_call_target="tpu_custom_call" | custom-call | tf_op jit(solution)/shard_map/pallas_call | solution.py:549

commit v7 on v5

--- a/solution.py
+++ b/solution.py
@@ -99,6 +99,14 @@
     has_rim = jnp.logical_and(core == 1, g < last)
     gives_rim = jnp.logical_and(core == 0, g > 0)
 
+    loads = [
+        pltpu.make_async_copy(grad_hbm, grad_ref, local.at[0]),
+        pltpu.make_async_copy(act_hbm, act_ref, local.at[1]),
+        pltpu.make_async_copy(weight_hbm, weight_ref, local.at[2]),
+    ]
+    for c in loads:
+        c.start()
+
     barrier = pltpu.get_barrier_semaphore()
     near = [at_chan(1, 0), at_chan(3, 0), at_chan(0, 1), at_chan(1, 1), at_chan(3, 1), mate]
     far_first = [d for high in (NZ, 0) for k in (4, 3, 5, 2, 6, 1, 7, 0) for d in (k + high,) if d]
@@ -122,14 +130,6 @@
     @pl.when(g == 2 * NZ - 1)
     def _():
         pl.semaphore_signal(barrier, inc=1, device_id=(0, chan), device_id_type=MESH)
-
-    loads = [
-        pltpu.make_async_copy(grad_hbm, grad_ref, local.at[0]),
-        pltpu.make_async_copy(act_hbm, act_ref, local.at[1]),
-        pltpu.make_async_copy(weight_hbm, weight_ref, local.at[2]),
-    ]
-    for c in loads:
-        c.start()
 
     def piece(plane, dx, dy, h):
         start = pl.multiple_of(chan_of(dx, dy) * 32 + 16 * h, 16)

time: 45.2 us -> 45.3 us (level)
  no operation moved by 1% of the time
where the time goes in v7:
time: 45.3 us; the launch traced here: 45.2 us
  Pallas kernels  44.5 us (98%)
  between operations  0.64 us (1%)
    pallas_call x1, Pallas kernels, on_device(): pl.pallas_call(lambda *refs: kernel(norm, *refs), out_shape=(maps, jax.Sh...  42.8 us
    pallas_call x1, Pallas kernels, on_device(): pl.pallas_call(finish, out_shape=(maps, jax.ShapeDtypeStruct(weight.shape...  1.7 us

profile of v7, /device:TPU:1, one launch (start us, length us, event | category | flops | bytes accessed | tf_op | source)
XLA Modules:
  0.0 45.2 jit_solution(11186133848638865819)
XLA Ops:
  0.6 42.8 %shard_map.50 = (bf16[32,1,8,16,128]{4,3,2,1,0:T(8,128)(2,1)S(1)}, bf16[2,2,16,2,16,128]{5,4,3,2,1,0:T(8,128)(2,1)S(1)}) custom-call(bf16[32,1,8,16,128]{4,3,2,1,0:T(8,128)(2,1)} %refs_0_.1, bf16[32,1,16,128]{3,2,1,0:T(8,128)(2,1)} %refs_1_.1, bf16[27,32,256]{2,1,0:T(8,128)(2,1)} %refs_2_.1), custom_call_target="tpu_custom_call" | custom-call | tf_op jit(solution)/shard_map/pallas_call | solution.py:515
  43.5 1.7 %shard_map.51 = (bf16[32,1,8,16,128]{4,3,2,1,0:T(8,128)(2,1)}, f32[27,32,256]{2,1,0:T(8,128)}) custom-call(bf16[2,2,16,2,16,128]{5,4,3,2,1,0:T(8,128)(2,1)S(1)} %get-tuple-element.4.codes, bf16[32,1,8,16,128]{4,3,2,1,0:T(8,128)(2,1)S(1)} %get-tuple-element.5.act_ref), custom_call_target="tpu_custom_call" | custom-call | tf_op jit(solution)/shard_map/pallas_call | solution.py:543
